TPU v7x, 128 devices: a whole 4x4x4 slice. The times are simulated.
128 devices in a mesh: dp: 2 (over core), vocab: 64 (over z, y, x).
Axes of the slice: x: 4, y: 4, z: 4, core: 2. Of those that a mesh axis runs over, the one named last changes fastest.
Arguments:
- hidden: bfloat16 [384, 8192], P('dp', 'vocab'), may hold values from -12 to 12
- tangent_hidden: bfloat16 [384, 8192], P('dp', 'vocab'), may hold values from -6 to 6
- head: bfloat16 [8192, 65536], P('dp', 'vocab'), may hold values from -1 to 1
- tangent_head: bfloat16 [8192, 65536], P('dp', 'vocab'), may hold values from -0.0625 to 0.0625
- allowed: int32 [384, 512], P('dp', 'vocab'), may hold values from 0 to 1, as said below
Outputs:
- head_product: bfloat16 [8192, 65536], P('dp', 'vocab')
- hidden_product: bfloat16 [384, 8192], P('dp', 'vocab')
Inputs may be any that keep to these rules, and one draw needn't show every extreme that they name: Every token allows block 0. The chance that a block is allowed rises along the vocabulary from about a tenth to about nine tenths.
All inputs are finite; a program needn't handle non-finite values.
Results may differ from a plain program's by a relative error of at most 0.012.
Values may be sent and summed in bfloat16 or wider, within the bound.
No kernel may reach another device: no remote copies, remote signals or barrier semaphores. Data moves between devices by JAX's collectives and lax.ppermute only.
A program may use at most 192 MiB of HBM per device.

v0:
```python
import functools

import jax
import jax.numpy as jnp
from jax import lax
from jax.experimental import pallas as pl
from jax.experimental.pallas import tpu as pltpu
from jax.sharding import PartitionSpec as P

AXES = ("dp", "vocab")
SIDE = 4
TOK = 192
COLS = 1024
NEG = -1e30
WHOLE = pl.BlockSpec(memory_space=pltpu.VMEM)
SCALARS = pl.BlockSpec(memory_space=pltpu.SMEM)
ORDER = [(s, q) for s in range(4) for q in range(2)]
F32 = jnp.float32
BF16 = jnp.bfloat16


def flat(k, z, y, x):
    return k * 64 + (z % 4) * 16 + (y % 4) * 4 + x % 4


def sites():
    return [(k, z, y, x) for k in range(2) for z in range(4) for y in range(4) for x in range(4)]


def last_shift(d):
    return [(flat(k, z, y, x), flat(k, z, y, x + d) if k == 1 else flat(k, z, y + d, x)) for k, z, y, x in sites()]


def mid_shift(d):
    return [(flat(k, z, y, x), flat(k, z, y + d, x) if k == 1 else flat(k, z, y, x + d)) for k, z, y, x in sites()]


def swap_pairs():
    return [(flat(k, z, y, x), flat(1 - k, z, y, x)) for k, z, y, x in sites()]


def start_pairs(c):
    return [(flat(k, z, y, x), flat(z // 2, 2 * k + z % 2 + c, y, x)) for k, z, y, x in sites()]


def plane_groups():
    return [[flat(1, r, m, x) for m in range(4) for r in range(4)] for x in range(4)] + [
        [flat(0, r, y, m) for m in range(4) for r in range(4)] for y in range(4)
    ]


def permute(value, pairs):
    return lax.ppermute(value, AXES, pairs)


def params(mib):
    return pltpu.CompilerParams(vmem_limit_bytes=mib << 20)


def cost(flops, moved):
    return pl.CostEstimate(flops=flops, bytes_accessed=moved, transcendentals=0)


def load_kernel(a, out, sem):
    copy = pltpu.make_async_copy(a, out, sem)
    copy.start()
    copy.wait()


def load_near(a, name):
    return pl.pallas_call(
        load_kernel,
        in_specs=[pl.BlockSpec(memory_space=pl.ANY)],
        out_specs=WHOLE,
        out_shape=pltpu.VMEM(a.shape, a.dtype),
        scratch_shapes=[pltpu.SemaphoreType.DMA],
        compiler_params=params(2),
        cost_estimate=cost(0, 24 << 20),
        name=name,
    )(pltpu.with_memory_space_constraint(a, pltpu.HBM))


def join_kernel(a, b, out, sems):
    copies = [
        pltpu.make_async_copy(a, out.at[0:TOK], sems.at[0]),
        pltpu.make_async_copy(b, out.at[TOK : 2 * TOK], sems.at[1]),
    ]
    for c in copies:
        c.start()
    for c in copies:
        c.wait()


def join(a, b):
    return pl.pallas_call(
        join_kernel,
        in_specs=[pl.BlockSpec(memory_space=pl.ANY)] * 2,
        out_specs=WHOLE,
        out_shape=jax.ShapeDtypeStruct((2 * TOK, 128), BF16),
        scratch_shapes=[pltpu.SemaphoreType.DMA((2,))],
        compiler_params=params(2),
        name="join",
    )(a, b)


def arrange_kernel(place, *refs):
    blocks, out = refs[:4], refs[4]
    for c in range(4):
        e = lax.rem(place[3] + 4 - c, 4)
        out[jnp.where(e // 2 == place[0], 0, 1), lax.rem(e, 2)] = blocks[c][...]


def arrange(place, blocks):
    return pl.pallas_call(
        arrange_kernel,
        in_specs=[SCALARS] + [WHOLE] * 4,
        out_specs=WHOLE,
        out_shape=jax.ShapeDtypeStruct((2, 2, 2 * TOK, 128), BF16),
        compiler_params=params(8),
        name="arrange",
    )(place, *blocks)


def rows_at(place, d, s, q, crossed=False):
    first, second = (place[2], place[1]) if crossed else (place[1], place[2])
    last, mid = lax.rem(first + 4 - d, 4), lax.rem(second + 4 - s, 4)
    r = jnp.where(place[0] == (0 if crossed else 1), 4 * mid + last, 4 * last + mid)
    return pl.ds(pl.multiple_of((16 * q + r) * 128, 128), 128)


def score_kernel(place, *refs, steps, added, final):
    n = len(steps)
    chunks, (head, thead), refs = refs[:n], refs[n : n + 2], refs[n + 2 :]
    early, refs = (refs[0], refs[1:]) if added else (None, refs)
    if final:
        got, allowed, weights, tangent, stats, acc = refs
    else:
        (acc,) = refs
    spots = [rows_at(place, d, s, q) for d in steps for s, q in ORDER]
    left = jnp.concatenate([c[s, q] for c in chunks for s, q in ORDER], axis=1)
    for n in range(4):
        cols = slice(256 * n, 256 * n + 256)
        right = jnp.concatenate([head[r, cols] for r in spots], axis=0)
        turn = jnp.concatenate([thead[r, cols] for r in spots], axis=0)
        both = jnp.dot(left, right, preferred_element_type=F32)
        more = jnp.dot(left[:TOK], turn, preferred_element_type=F32)
        if added:
            both = both + early[:, cols]
        acc[:TOK, cols] = both[:TOK]
        acc[TOK:, cols] = both[TOK:] + more
    if not final:
        return
    lane = lax.broadcasted_iota(jnp.int32, (32, 128), 1)
    ticket = jnp.concatenate([allowed[...].astype(F32), jnp.zeros((8, 64), F32)], axis=1)
    ticket = jnp.transpose(jnp.concatenate([ticket, jnp.zeros((120, 256), F32)], axis=0))
    parts = []
    for r in range(0, TOK, 32):
        rows, trows = slice(r, r + 32), slice(TOK + r, TOK + r + 32)
        logit = acc[rows, :] + got[rows, :]
        tang = acc[trows, :] + got[trows, :]
        ok = jnp.concatenate([jnp.broadcast_to(ticket[rows, b : b + 1], (32, 128)) for b in range(8)], axis=1) > 0.5
        logit = jnp.where(ok, logit, NEG)
        top = jnp.max(logit, axis=1, keepdims=True)
        w = jnp.where(ok, jnp.exp(logit - top), 0.0)
        den = jnp.sum(w, axis=1, keepdims=True)
        mom = jnp.sum(w * tang, axis=1, keepdims=True)
        weights[rows, :] = w
        tangent[rows, :] = tang
        parts.append(jnp.where(lane == 0, top, jnp.where(lane == 1, den, jnp.where(lane == 2, mom, 0.0))))
    first = jnp.concatenate(parts[:4], axis=0)
    second = jnp.concatenate(parts[4:] + [jnp.zeros((64, 128), F32)], axis=0)
    stats[0:4, :] = jnp.transpose(first)[0:4, :]
    stats[4:8, :] = jnp.transpose(second)[0:4, :]


def scores(place, steps, chunks, head, thead, name, weight, early=None, late=()):
    added, final = early is not None, len(late) > 0
    operands = [place, *chunks, head, thead, *([early] if added else []), *late]
    shapes = [(TOK, COLS), (TOK, COLS), (8, 128)] if final else [(2 * TOK, COLS)]
    out = pl.pallas_call(
        functools.partial(score_kernel, steps=steps, added=added, final=final),
        in_specs=[SCALARS] + [WHOLE] * (len(operands) - 1),
        out_specs=[WHOLE] * len(shapes),
        out_shape=[jax.ShapeDtypeStruct(s, F32) for s in shapes],
        scratch_shapes=[pltpu.VMEM((2 * TOK, COLS), F32)] if final else [],
        compiler_params=params(12),
        cost_estimate=cost(weight * 6 * TOK * 4096 * COLS, weight << 20),
        name=name,
    )(*operands)
    return out if final else out[0]


def product_kernel(every, mine, weights, tangent, out):
    cols = []
    for g in range(2):
        top = every[:, 4 * g, :]
        best = jnp.max(top, axis=0, keepdims=True)
        scale = jnp.exp(top - best)
        den = jnp.sum(every[:, 4 * g + 1, :] * scale, axis=0, keepdims=True)
        mom = jnp.sum(every[:, 4 * g + 2, :] * scale, axis=0, keepdims=True)
        if g:
            real = lax.broadcasted_iota(jnp.int32, (1, 128), 1) < 64
            den = jnp.where(real, den, 1.0)
        factor = jnp.exp(mine[4 * g : 4 * g + 1, :] - best) / den
        mean = mom / den
        row = lax.broadcasted_iota(jnp.int32, (128, 128), 0)
        cols.append(jnp.transpose(jnp.where(row == 0, factor, jnp.where(row == 1, mean, 0.0))))
    both = jnp.concatenate([cols[0], cols[1][:64]], axis=0)
    for r in range(0, TOK, 32):
        rows = slice(r, r + 32)
        p = (weights[rows, :] * both[rows, 0:1]) * (tangent[rows, :] - both[rows, 1:2])
        out[rows, :] = p.astype(BF16)


def make_product(every, mine, weights, tangent):
    return pl.pallas_call(
        product_kernel,
        in_specs=[WHOLE] * 4,
        out_specs=WHOLE,
        out_shape=jax.ShapeDtypeStruct((TOK, COLS), BF16),
        compiler_params=params(16),
        name="product",
    )(every, mine, weights, tangent)


def back_kernel(place, product, head, *refs, crossed):
    outs, turned = refs[:4], refs[4]
    turned[...] = jnp.transpose(product[...].astype(F32)).astype(BF16)
    for d in (1, 3, 2, 0):
        rows = jnp.concatenate([head[rows_at(place, d, s, q, crossed), :] for s, q in ORDER], axis=0)
        term = jnp.dot(rows, turned[...], preferred_element_type=F32).astype(BF16)
        for s in range(4):
            low, high = term[256 * s : 256 * s + 128], term[256 * s + 128 : 256 * s + 256]
            outs[d][s, 0] = low[:, :128]
            outs[d][s, 1] = high[:, :128]
            outs[d][s, 2] = jnp.concatenate([low[:, 128:], high[:, 128:]], axis=1)


def back(place, product, head, crossed, name):
    return pl.pallas_call(
        functools.partial(back_kernel, crossed=crossed),
        in_specs=[SCALARS, WHOLE, WHOLE],
        out_specs=[WHOLE] * 4,
        out_shape=[jax.ShapeDtypeStruct((4, 3, 128, 128), BF16)] * 4,
        scratch_shapes=[pltpu.VMEM((COLS, TOK), BF16)],
        compiler_params=params(8),
        cost_estimate=cost(2 * TOK * 4096 * COLS, 10 << 20),
        name=name,
    )(place, product, head)


def added(terms, s, b):
    value = terms[0][s, b].astype(F32)
    for term in terms[1:]:
        value = value + term[s, b].astype(F32)
    return value.astype(BF16)


def line_sum_kernel(*refs):
    terms, out = refs[:4], refs[4]
    for s in range(4):
        for b in range(3):
            out[s, b] = added(terms, s, b)


def line_sum(terms):
    return pl.pallas_call(
        line_sum_kernel,
        in_specs=[WHOLE] * 4,
        out_specs=WHOLE,
        out_shape=jax.ShapeDtypeStruct((4, 3, 128, 128), BF16),
        compiler_params=params(10),
        name="line_sum",
    )(*terms)


def pack_kernel(place, *refs):
    terms, got, out = refs[:4], refs[4], refs[5]
    for s in range(4):
        mid = lax.rem(place[2] + 4 - s, 4)
        for t in range(2):
            half = jnp.where(place[0] == t, 0, 1)
            sums = [got[s, b] if t else added(terms, s, b) for b in range(3)]
            for q in range(2):
                tail = sums[2][:, 64 * q : 64 * q + 64]
                to = 4 * mid + 2 * half + q
                out[to, 0:128] = sums[q]
                out[to, 128:TOK] = jnp.concatenate([tail[:64], tail[64:]], axis=1)


def pack(place, terms, got):
    return pl.pallas_call(
        pack_kernel,
        in_specs=[SCALARS] + [WHOLE] * 5,
        out_specs=WHOLE,
        out_shape=jax.ShapeDtypeStruct((16, TOK, 128), BF16),
        compiler_params=params(10),
        name="pack",
    )(place, *terms, got)


def plane_sum_kernel(terms, out):
    value = terms[0].astype(F32)
    for j in range(1, 16):
        value = value + terms[j].astype(F32)
    fold = value[128:]
    out[0:128] = jnp.transpose(value[:128]).astype(BF16)
    tail = jnp.concatenate([fold[:, :64], fold[:, 64:]], axis=0)
    out[128:TOK] = jnp.transpose(tail).astype(BF16)


def plane_sum(terms):
    return pl.pallas_call(
        plane_sum_kernel,
        in_specs=[WHOLE],
        out_specs=WHOLE,
        out_shape=jax.ShapeDtypeStruct((TOK, 128), BF16),
        compiler_params=params(8),
        name="plane_sum",
    )(terms)


def outer_kernel(place, *refs):
    mine, others, p_own, p_other, out, held = refs[:4], refs[4:8], refs[8], refs[9], refs[10], refs[11]
    i = pl.program_id(0)

    @pl.when(i == 0)
    def _():
        for d in range(4):
            for s, q in ORDER:
                rows = rows_at(place, d, s, q)
                held[rows.start // 128, 0:TOK] = mine[d][s, q]
                held[rows.start // 128, TOK : 2 * TOK] = others[d][s, q]

    left = jnp.concatenate([held[4 * i + j] for j in range(4)], axis=1)
    right = jnp.concatenate([p_own[...], p_other[...]], axis=0)
    out[...] = lax.dot_general(left, right, (((0,), (0,)), ((), ())), preferred_element_type=F32).astype(BF16)


def outer(place, mine, others, p_own, p_other):
    rows = pl.BlockSpec((4, 2, TOK, 128), lambda i: (0, 0, 0, 0))
    whole = pl.BlockSpec((TOK, COLS), lambda i: (0, 0))
    return pl.pallas_call(
        outer_kernel,
        grid=(8,),
        in_specs=[SCALARS] + [rows] * 8 + [whole] * 2,
        out_specs=pl.BlockSpec((512, COLS), lambda i: (i, 0)),
        out_shape=jax.ShapeDtypeStruct((4096, COLS), BF16),
        scratch_shapes=[pltpu.VMEM((32, 2 * TOK, 128), BF16)],
        compiler_params=params(16),
        cost_estimate=cost(4 * TOK * 4096 * COLS, 12 << 20),
        name="head_outer",
    )(place, *mine, *others, p_own, p_other)


def shards(hidden, tangent_hidden, head, tangent_head, allowed):
    k, v = lax.axis_index("dp"), lax.axis_index("vocab")
    z, y, x = v // 16, (v // 4) % 4, v % 4
    place = jnp.stack([k, jnp.where(k == 1, x, y), jnp.where(k == 1, y, x), z]).astype(jnp.int32)
    rows = join(*(pltpu.with_memory_space_constraint(h, pltpu.HBM) for h in (hidden, tangent_hidden)))
    both = arrange(place, [permute(rows, start_pairs(c)) for c in range(4)])
    middle = [both] + [permute(both, mid_shift(s)) for s in (1, 2, 3)]
    head, middle[1] = lax.optimization_barrier((head, middle[1]))
    head_near = load_near(head, "load_head")
    middle[2], head_near = lax.optimization_barrier((middle[2], head_near))
    own = jnp.stack([m[0] for m in middle])
    other = jnp.stack([m[1] for m in middle])
    other1, other3, own3 = permute(other, last_shift(1)), permute(other, last_shift(-1)), permute(own, last_shift(-1))
    other2 = permute(other1, last_shift(1))
    tangent_head, _ = lax.optimization_barrier((tangent_head, other1))
    near = (head_near, load_near(tangent_head, "load_tangent"))
    early = scores(place, (0, 1), [other, other1], *near, "other_first", 0)
    own, other3, own3, early = lax.optimization_barrier((own, other3, own3, early))
    own2, own1 = permute(own3, last_shift(-1)), permute(own, last_shift(1))
    owns, others = [own, own1, own2, own3], [other, other1, other2, other3]

    sent = scores(place, (3, 2), [other3, other2], *near, "other_last", 10, early)
    got = permute(sent, swap_pairs())
    early = scores(place, (0, 3), [own, own3], *near, "own_first", 10)
    late = (got, jnp.transpose(allowed))
    early = scores(place, (2,), [own2], *near, "own_next", 0, early)
    weights, tangent, stats = scores(place, (1,), [own1], *near, "own_last", 0, early, late)
    every = lax.all_to_all(
        jnp.broadcast_to(stats[None], (64, 8, 128)), "vocab", split_axis=0, concat_axis=0, tiled=True
    )
    p_own = make_product(every, stats, weights, tangent)
    p_other = permute(p_own, swap_pairs())

    terms = back(place, p_own, head_near, False, "back_own")
    mine = [terms[0]] + [permute(terms[d], last_shift(-d)) for d in (1, 3)]
    across = back(place, p_other, head_near, True, "back_other")
    theirs = [across[0]] + [permute(across[d], mid_shift(-d)) for d in (1, 3, 2)]
    term, _ = lax.optimization_barrier((terms[2], across[0]))
    mine.append(permute(term, last_shift(-2)))
    p_own, theirs[1] = lax.optimization_barrier((p_own, theirs[1]))
    head_product = outer(place, owns, others, p_own, p_other)
    head_product, theirs[0] = lax.optimization_barrier((head_product, theirs[0]))
    rest = permute(line_sum(theirs), swap_pairs())
    slab = pack(place, mine, rest)
    arrived = lax.all_to_all(slab, AXES, split_axis=0, concat_axis=0, tiled=True, axis_index_groups=plane_groups())
    hidden_product = plane_sum(arrived)
    return head_product, hidden_product


def solution(mesh):
    place = P("dp", "vocab")
    return jax.shard_map(shards, mesh=mesh, in_specs=(place,) * 5, out_specs=(place, place), check_vma=False)
```

profile of v0, /device:TPU:1, one launch (start us, length us, event | category | flops | bytes accessed | tf_op | source)
XLA Modules:
  0.0 133.5 jit_solution(10160616629171707060)
XLA Ops:
  0.6 0.8 join.1
  1.5 6.9 %collective-permute-start = (bf16[384,128]{1,0:T(8,128)(2,1)S(1)}, bf16[384,128]{1,0:T(8,128)(2,1)S(1)}, u32[]{:S(2)}, u32[]{:S(2)}) collective-permute-start(bf16[384,128]{1,0:T(8,128)(2,1)S(1)} %join.1), channel_id=1, source_target_pairs={{0,0},{1,1},{2,2},{3,3},{4,4},{5,5},{6,6},{7,7},{8,8},{9,9},{10,10... | collective-permute-start | bytes 294920 | tf_op jit(solution)/shard_map/ppermute | solution.py:53
  8.4 0.2 collective-permute-start.1
  8.6 0.9 collective-permute-start.3
  9.6 1.4 %collective-permute-done.refs_0_ = bf16[384,128]{1,0:T(8,128)(2,1)S(1)} collective-permute-done((bf16[384,128]{1,0:T(8,128)(2,1)S(1)}, bf16[384,128]{1,0:T(8,128)(2,1)S(1)}, u32[]{:S(2)}, u32[]{:S(2)}) %collective-permute-start) | collective-permute-done | bytes 98336 | tf_op jit(solution)/shard_map/ppermute | solution.py:53
  11.0 3.7 %collective-permute-done.1.refs_1_ = bf16[384,128]{1,0:T(8,128)(2,1)S(1)} collective-permute-done((bf16[384,128]{1,0:T(8,128)(2,1)S(1)}, bf16[384,128]{1,0:T(8,128)(2,1)S(1)}, u32[]{:S(2)}, u32[]{:S(2)}) %collective-permute-start.1) | collective-permute-done | bytes 98336 | tf_op jit(solution)/shard_map/ppermute | solution.py:53
  14.7 0.5 collective-permute-done.3.refs_3_
  15.2 0.6 arrange.1
  15.8 1.4 %collective-permute-start.4 = (bf16[2,2,384,128]{3,2,1,0:T(8,128)(2,1)S(1)}, bf16[2,2,384,128]{3,2,1,0:T(8,128)(2,1)S(1)}, u32[]{:S(2)}, u32[]{:S(2)}) collective-permute-start(bf16[2,2,384,128]{3,2,1,0:T(8,128)(2,1)S(1)} %arrange.1), channel_id=1, source_target_pairs={{0,1},{1,2},{2,3},{3,0},{4,5},{5,6},{6,7},{7,4},{8,9},{9,10},{10,1... | collective-permute-start | bytes 1179656 | tf_op jit(solution)/shard_map/ppermute | solution.py:53
  17.2 2.6 %collective-permute-start.5 = (bf16[2,2,384,128]{3,2,1,0:T(8,128)(2,1)S(1)}, bf16[2,2,384,128]{3,2,1,0:T(8,128)(2,1)S(1)}, u32[]{:S(2)}, u32[]{:S(2)}) collective-permute-start(bf16[2,2,384,128]{3,2,1,0:T(8,128)(2,1)S(1)} %arrange.1), channel_id=1, source_target_pairs={{0,2},{1,3},{2,0},{3,1},{4,6},{5,7},{6,4},{7,5},{8,10},{9,11},{10,... | collective-permute-start | bytes 1179656 | tf_op jit(solution)/shard_map/ppermute | solution.py:53
  19.8 1.1 collective-permute-start.6
  20.9 3.2 %collective-permute-done.4 = bf16[2,2,384,128]{3,2,1,0:T(8,128)(2,1)S(1)} collective-permute-done((bf16[2,2,384,128]{3,2,1,0:T(8,128)(2,1)S(1)}, bf16[2,2,384,128]{3,2,1,0:T(8,128)(2,1)S(1)}, u32[]{:S(2)}, u32[]{:S(2)}) %collective-permute-start.4) | collective-permute-done | bytes 393248 | tf_op jit(solution)/shard_map/ppermute | solution.py:53
  24.1 3.4 %load_head.1.refs_2_.refs_1_.head = bf16[4096,1024]{1,0:T(8,128)(2,1)S(1)} custom-call(bf16[4096,1024]{1,0:T(8,128)(2,1)} %a.2), custom_call_target="tpu_custom_call" | custom-call | bytes 25165824 | tf_op jit(solution)/shard_map/load_head/pallas_call | solution.py:71
  27.5 2.0 %collective-permute-done.5 = bf16[2,2,384,128]{3,2,1,0:T(8,128)(2,1)S(1)} collective-permute-done((bf16[2,2,384,128]{3,2,1,0:T(8,128)(2,1)S(1)}, bf16[2,2,384,128]{3,2,1,0:T(8,128)(2,1)S(1)}, u32[]{:S(2)}, u32[]{:S(2)}) %collective-permute-start.5) | collective-permute-done | bytes 393248 | tf_op jit(solution)/shard_map/ppermute | solution.py:53
  29.7 1.0 collective-permute-start.9
  30.7 1.8 %collective-permute-start.7 = (bf16[4,2,384,128]{3,2,1,0:T(8,128)(2,1)S(1)}, bf16[4,2,384,128]{3,2,1,0:T(8,128)(2,1)S(1)}, u32[]{:S(2)}, u32[]{:S(2)}) collective-permute-start(bf16[4,2,384,128]{3,2,1,0:T(8,128)(2,1)S(1)} %pad_maximum_fusion.1.refs_0_.refs_4_), channel_id=1, source_target_pairs={{0,12},{1,13},{2,14},{3,15},{4,0},{5,1},{6,2},{7,3},{8,4},{9,5},{1... | collective-permute-start | bytes 2359304 | tf_op jit(solution)/shard_map/ppermute | solution.py:53
  32.5 1.0 collective-permute-start.8
  33.6 8.5 %collective-permute-done.9.refs_1_.refs_5_ = bf16[4,2,384,128]{3,2,1,0:T(8,128)(2,1)S(1)} collective-permute-done((bf16[4,2,384,128]{3,2,1,0:T(8,128)(2,1)S(1)}, bf16[4,2,384,128]{3,2,1,0:T(8,128)(2,1)S(1)}, u32[]{:S(2)}, u32[]{:S(2)}) %collective-permute-start.9) | collective-permute-done | bytes 786464 | tf_op jit(solution)/shard_map/ppermute | solution.py:53
  42.1 3.4 %load_tangent.1.refs_3_.refs_2_ = bf16[4096,1024]{1,0:T(8,128)(2,1)S(1)} custom-call(bf16[4096,1024]{1,0:T(8,128)(2,1)} %a.3), custom_call_target="tpu_custom_call" | custom-call | bytes 25165824 | tf_op jit(solution)/shard_map/load_tangent/pallas_call | solution.py:71
  45.5 3.2 %other_first.1.refs_4_ = f32[384,1024]{1,0:T(8,128)S(1)} custom-call(s32[4]{0:T(128)S(1)} %pad_add_fusion.place, bf16[4,2,384,128]{3,2,1,0:T(8,128)(2,1)S(1)} %pad_maximum_fusion.1.refs_0_.refs_4_, bf16[4,2,384,128]{3,2,1,0:T(8,128)(2,1)S(1)} %collective-permute-done.9.refs_1_.refs_5_, bf16[4096,1024]{1,0:T(8,128)(2,1)S(1)} %load_head.1.refs_2_.refs_1_.head, ...), custom_call_target="tpu_custom_call" | custom-call | tf_op jit(solution)/shard_map/other_first/pallas_call | solution.py:180
  48.7 1.6 %collective-permute-done.8.refs_1_.refs_3_ = bf16[4,2,384,128]{3,2,1,0:T(8,128)(2,1)S(1)} collective-permute-done((bf16[4,2,384,128]{3,2,1,0:T(8,128)(2,1)S(1)}, bf16[4,2,384,128]{3,2,1,0:T(8,128)(2,1)S(1)}, u32[]{:S(2)}, u32[]{:S(2)}) %collective-permute-start.8) | collective-permute-done | bytes 786464 | tf_op jit(solution)/shard_map/ppermute | solution.py:53
  50.2 3.0 %collective-permute-start.11 = (bf16[4,2,384,128]{3,2,1,0:T(8,128)(2,1)S(1)}, bf16[4,2,384,128]{3,2,1,0:T(8,128)(2,1)S(1)}, u32[]{:S(2)}, u32[]{:S(2)}) collective-permute-start(bf16[4,2,384,128]{3,2,1,0:T(8,128)(2,1)S(1)} %collective-permute-done.8.refs_1_.refs_3_), channel_id=1, source_target_pairs={{0,12},{1,13},{2,14},{3,15},{4,0},{5,1},{6,2},{7,3},{8,4},{9,5},{1... | collective-permute-start | bytes 2359304 | tf_op jit(solution)/shard_map/ppermute | solution.py:53
  53.2 1.2 collective-permute-done.12.refs_1_.refs_6_
  54.5 3.2 %other_last.1 = f32[384,1024]{1,0:T(8,128)S(1)} custom-call(s32[4]{0:T(128)S(1)} %pad_add_fusion.place, bf16[4,2,384,128]{3,2,1,0:T(8,128)(2,1)S(1)} %collective-permute-done.7.refs_0_.refs_7_, bf16[4,2,384,128]{3,2,1,0:T(8,128)(2,1)S(1)} %collective-permute-done.12.refs_1_.refs_6_, bf16[4096,1024]{1,0:T(8,128)(2,1)S(1)} %load_head.1.refs_2_.refs_1_.head, ...), custom_call_target="tpu_custom_call" | custom-call | flops 48318382080 | bytes 10485760 | tf_op jit(solution)/shard_map/other_last/pallas_call | solution.py:180
  57.6 3.6 %collective-permute-start.13 = (f32[384,1024]{1,0:T(8,128)S(1)}, f32[384,1024]{1,0:T(8,128)S(1)}, u32[]{:S(2)}, u32[]{:S(2)}) collective-permute-start(f32[384,1024]{1,0:T(8,128)S(1)} %other_last.1), channel_id=1, source_target_pairs={{0,64},{1,65},{2,66},{3,67},{4,68},{5,69},{6,70},{7,71},{8,72},{9,... | collective-permute-start | bytes 4718600 | tf_op jit(solution)/shard_map/ppermute | solution.py:53
  61.2 3.2 %own_first.1.refs_3_ = f32[384,1024]{1,0:T(8,128)S(1)} custom-call(s32[4]{0:T(128)S(1)} %pad_add_fusion.place, bf16[4,2,384,128]{3,2,1,0:T(8,128)(2,1)S(1)} %pad_maximum_fusion.refs_0_, bf16[4,2,384,128]{3,2,1,0:T(8,128)(2,1)S(1)} %collective-permute-done.8.refs_1_.refs_3_, bf16[4096,1024]{1,0:T(8,128)(2,1)S(1)} %load_head.1.refs_2_.refs_1_.head, ...), custom_call_target="tpu_custom_call" | custom-call | flops 48318382080 | bytes 10485760 | tf_op jit(solution)/shard_map/own_first/pallas_call | solution.py:180
  64.4 1.9 %own_next.1.refs_3_ = f32[384,1024]{1,0:T(8,128)S(1)} custom-call(s32[4]{0:T(128)S(1)} %pad_add_fusion.place, bf16[4,2,384,128]{3,2,1,0:T(8,128)(2,1)S(1)} %collective-permute-done.11.refs_0_.refs_2_, bf16[4096,1024]{1,0:T(8,128)(2,1)S(1)} %load_head.1.refs_2_.refs_1_.head, bf16[4096,1024]{1,0:T(8,128)(2,1)S(1)} %load_tangent.1.refs_3_.refs_2_, ...), custom_call_target="tpu_custom_call" | custom-call | tf_op jit(solution)/shard_map/own_next/pallas_call | solution.py:180
  66.4 2.4 %own_last.1 = (f32[192,1024]{1,0:T(8,128)S(1)}, f32[192,1024]{1,0:T(8,128)S(1)}, f32[8,128]{1,0:T(8,128)S(1)}) custom-call(s32[4]{0:T(128)S(1)} %pad_add_fusion.place, bf16[4,2,384,128]{3,2,1,0:T(8,128)(2,1)S(1)} %collective-permute-done.10.refs_0_.refs_1_, bf16[4096,1024]{1,0:T(8,128)(2,1)S(1)} %load_head.1.refs_2_.refs_1_.head, ...), custom_call_target="tpu_custom_call" | custom-call | tf_op jit(solution)/shard_map/own_last/pallas_call | solution.py:180
  68.9 16.4 %all_to_all.10.every = f32[64,8,128]{2,1,0:T(8,128)S(1)} all-to-all(f32[64,8,128]{2,1,0:T(8,128)S(1)} %broadcast_in_dim.2), channel_id=1, replica_groups=mesh['dp'=2,'vocab'=64] {'vocab'}, dimensions={0} | all-to-all | bytes 524288 | tf_op jit(solution)/shard_map/all_to_all | solution.py:383
  85.3 0.4 product.1.refs_8_
  85.7 4.6 %collective-permute-start.14 = (bf16[192,1024]{1,0:T(8,128)(2,1)S(1)}, bf16[192,1024]{1,0:T(8,128)(2,1)S(1)}, u32[]{:S(2)}, u32[]{:S(2)}) collective-permute-start(bf16[192,1024]{1,0:T(8,128)(2,1)S(1)} %product.1.refs_8_), channel_id=1, source_target_pairs={{0,64},{1,65},{2,66},{3,67},{4,68},{5,69},{6,70},{7,71},{8,72},{9,... | collective-permute-start | bytes 1179656 | tf_op jit(solution)/shard_map/ppermute | solution.py:53
  90.4 1.3 %collective-permute-done.14.product.refs_9_ = bf16[192,1024]{1,0:T(8,128)(2,1)S(1)} collective-permute-done((bf16[192,1024]{1,0:T(8,128)(2,1)S(1)}, bf16[192,1024]{1,0:T(8,128)(2,1)S(1)}, u32[]{:S(2)}, u32[]{:S(2)}) %collective-permute-start.14) | collective-permute-done | bytes 393248 | tf_op jit(solution)/shard_map/ppermute | solution.py:53
  91.7 3.1 %back_other.1 = (bf16[4,3,128,128]{3,2,1,0:T(8,128)(2,1)S(1)}, bf16[4,3,128,128]{3,2,1,0:T(8,128)(2,1)S(1)}, bf16[4,3,128,128]{3,2,1,0:T(8,128)(2,1)S(1)}, bf16[4,3,128,128]{3,2,1,0:T(8,128)(2,1)S(1)}) custom-call(s32[4]{0:T(128)S(1)} %pad_add_fusion.place, bf16[192,1024]{1,0:T(8,128)(2,1)S(1)} %collective-permute-done.14.product.refs_9_, ...), custom_call_target="tpu_custom_call" | custom-call | flops 1610612736 | bytes 10485760 | tf_op jit(solution)/shard_map/back_other/pallas_call | solution.py:240
  94.8 0.5 collective-permute-start.15
  95.3 1.1 collective-permute-start.19
  96.3 0.6 collective-permute-start.20
  97.0 3.1 %back_own.1 = (bf16[4,3,128,128]{3,2,1,0:T(8,128)(2,1)S(1)}, bf16[4,3,128,128]{3,2,1,0:T(8,128)(2,1)S(1)}, bf16[4,3,128,128]{3,2,1,0:T(8,128)(2,1)S(1)}, bf16[4,3,128,128]{3,2,1,0:T(8,128)(2,1)S(1)}) custom-call(s32[4]{0:T(128)S(1)} %pad_add_fusion.place, bf16[192,1024]{1,0:T(8,128)(2,1)S(1)} %product.1.refs_8_, ...), custom_call_target="tpu_custom_call" | custom-call | flops 1610612736 | bytes 10485760 | tf_op jit(solution)/shard_map/back_own/pallas_call | solution.py:240
  100.1 1.2 collective-permute-start.16
  101.3 0.3 collective-permute-start.17
  101.6 0.2 collective-permute-done.15.refs_1_
  101.8 0.9 collective-permute-start.18
  102.7 8.5 %head_outer.1 = bf16[4096,1024]{1,0:T(8,128)(2,1)} custom-call(s32[4]{0:T(128)S(1)} %pad_add_fusion.place, bf16[4,2,384,128]{3,2,1,0:T(8,128)(2,1)S(1)} %pad_maximum_fusion.refs_0_, bf16[4,2,384,128]{3,2,1,0:T(8,128)(2,1)S(1)} %collective-permute-done.10.refs_0_.refs_1_, bf16[4,2,384,128]{3,2,1,0:T(8,128)(2,1)S(1)} %collective-permute-done.11.refs_0_.refs_2_, ...), custom_call_target="tpu_custom_call" | custom-call | flops 3221225472 | bytes 12582912 | tf_op jit(solution)/shard_map/head_outer/pallas_call | solution.py:343
  111.2 0.2 line_sum.1
  111.4 1.9 %collective-permute-start.21 = (bf16[4,3,128,128]{3,2,1,0:T(8,128)(2,1)S(1)}, bf16[4,3,128,128]{3,2,1,0:T(8,128)(2,1)S(1)}, u32[]{:S(2)}, u32[]{:S(2)}) collective-permute-start(bf16[4,3,128,128]{3,2,1,0:T(8,128)(2,1)S(1)} %line_sum.1), channel_id=1, source_target_pairs={{0,64},{1,65},{2,66},{3,67},{4,68},{5,69},{6,70},{7,71},{8,72},{9,... | collective-permute-start | bytes 1179656 | tf_op jit(solution)/shard_map/ppermute | solution.py:53
  113.3 3.8 %collective-permute-done.17.refs_2_ = bf16[4,3,128,128]{3,2,1,0:T(8,128)(2,1)S(1)} collective-permute-done((bf16[4,3,128,128]{3,2,1,0:T(8,128)(2,1)S(1)}, bf16[4,3,128,128]{3,2,1,0:T(8,128)(2,1)S(1)}, u32[]{:S(2)}, u32[]{:S(2)}) %collective-permute-start.17) | collective-permute-done | bytes 393248 | tf_op jit(solution)/shard_map/ppermute | solution.py:53
  117.1 0.8 pack.1
  117.9 14.8 %all_to_all.11.terms = bf16[16,192,128]{2,1,0:T(8,128)(2,1)S(1)} all-to-all(bf16[16,192,128]{2,1,0:T(8,128)(2,1)S(1)} %pack.1), channel_id=1, replica_groups={{64,80,96,112,68,84,100,116,72,88,104,120,76,92,108,124},{65,81,97,113,..., dimensions={0} | all-to-all | bytes 1572864 | tf_op jit(solution)/shard_map/all_to_all | solution.py:400
  132.7 0.8 plane_sum.1
  (23 shorter events, 0.5 us)
Async XLA Ops:
  1.5 9.6 %collective-permute-start = (bf16[384,128]{1,0:T(8,128)(2,1)S(1)}, bf16[384,128]{1,0:T(8,128)(2,1)S(1)}, u32[]{:S(2)}, u32[]{:S(2)}) collective-permute-start(bf16[384,128]{1,0:T(8,128)(2,1)S(1)} %join.1), channel_id=1, source_target_pairs={{0,0},{1,1},{2,2},{3,3},{4,4},{5,5},{6,6},{7,7},{8,8},{9,9},{10,10... | collective-permute-start | bytes 294920 | tf_op jit(solution)/shard_map/ppermute | solution.py:53
  8.4 6.3 %collective-permute-start.1 = (bf16[384,128]{1,0:T(8,128)(2,1)S(1)}, bf16[384,128]{1,0:T(8,128)(2,1)S(1)}, u32[]{:S(2)}, u32[]{:S(2)}) collective-permute-start(bf16[384,128]{1,0:T(8,128)(2,1)S(1)} %join.1), channel_id=1, source_target_pairs={{0,16},{1,17},{2,18},{3,19},{4,20},{5,21},{6,22},{7,23},{8,24},{9,... | collective-permute-start | bytes 294920 | tf_op jit(solution)/shard_map/ppermute | solution.py:53
  8.6 6.1 %collective-permute-start.2 = (bf16[384,128]{1,0:T(8,128)(2,1)S(1)}, bf16[384,128]{1,0:T(8,128)(2,1)S(1)}, u32[]{:S(2)}, u32[]{:S(2)}) collective-permute-start(bf16[384,128]{1,0:T(8,128)(2,1)S(1)} %join.1), channel_id=1, source_target_pairs={{0,32},{1,33},{2,34},{3,35},{4,36},{5,37},{6,38},{7,39},{8,40},{9,... | collective-permute-start | bytes 294920 | tf_op jit(solution)/shard_map/ppermute | solution.py:53
  8.6 6.6 %collective-permute-start.3 = (bf16[384,128]{1,0:T(8,128)(2,1)S(1)}, bf16[384,128]{1,0:T(8,128)(2,1)S(1)}, u32[]{:S(2)}, u32[]{:S(2)}) collective-permute-start(bf16[384,128]{1,0:T(8,128)(2,1)S(1)} %join.1), channel_id=1, source_target_pairs={{0,48},{1,49},{2,50},{3,51},{4,52},{5,53},{6,54},{7,55},{8,56},{9,... | collective-permute-start | bytes 294920 | tf_op jit(solution)/shard_map/ppermute | solution.py:53
  15.8 8.3 %collective-permute-start.4 = (bf16[2,2,384,128]{3,2,1,0:T(8,128)(2,1)S(1)}, bf16[2,2,384,128]{3,2,1,0:T(8,128)(2,1)S(1)}, u32[]{:S(2)}, u32[]{:S(2)}) collective-permute-start(bf16[2,2,384,128]{3,2,1,0:T(8,128)(2,1)S(1)} %arrange.1), channel_id=1, source_target_pairs={{0,1},{1,2},{2,3},{3,0},{4,5},{5,6},{6,7},{7,4},{8,9},{9,10},{10,1... | collective-permute-start | bytes 1179656 | tf_op jit(solution)/shard_map/ppermute | solution.py:53
  17.2 12.3 %collective-permute-start.5 = (bf16[2,2,384,128]{3,2,1,0:T(8,128)(2,1)S(1)}, bf16[2,2,384,128]{3,2,1,0:T(8,128)(2,1)S(1)}, u32[]{:S(2)}, u32[]{:S(2)}) collective-permute-start(bf16[2,2,384,128]{3,2,1,0:T(8,128)(2,1)S(1)} %arrange.1), channel_id=1, source_target_pairs={{0,2},{1,3},{2,0},{3,1},{4,6},{5,7},{6,4},{7,5},{8,10},{9,11},{10,... | collective-permute-start | bytes 1179656 | tf_op jit(solution)/shard_map/ppermute | solution.py:53
  19.8 9.7 %collective-permute-start.6 = (bf16[2,2,384,128]{3,2,1,0:T(8,128)(2,1)S(1)}, bf16[2,2,384,128]{3,2,1,0:T(8,128)(2,1)S(1)}, u32[]{:S(2)}, u32[]{:S(2)}) collective-permute-start(bf16[2,2,384,128]{3,2,1,0:T(8,128)(2,1)S(1)} %arrange.1), channel_id=1, source_target_pairs={{0,3},{1,0},{2,1},{3,2},{4,7},{5,4},{6,5},{7,6},{8,11},{9,8},{10,9... | collective-permute-start | bytes 1179656 | tf_op jit(solution)/shard_map/ppermute | solution.py:53
  29.7 12.4 %collective-permute-start.9 = (bf16[4,2,384,128]{3,2,1,0:T(8,128)(2,1)S(1)}, bf16[4,2,384,128]{3,2,1,0:T(8,128)(2,1)S(1)}, u32[]{:S(2)}, u32[]{:S(2)}) collective-permute-start(bf16[4,2,384,128]{3,2,1,0:T(8,128)(2,1)S(1)} %pad_maximum_fusion.1.refs_0_.refs_4_), channel_id=1, source_target_pairs={{0,4},{1,5},{2,6},{3,7},{4,8},{5,9},{6,10},{7,11},{8,12},{9,13},{1... | collective-permute-start | bytes 2359304 | tf_op jit(solution)/shard_map/ppermute | solution.py:53
  30.7 18.0 %collective-permute-start.7 = (bf16[4,2,384,128]{3,2,1,0:T(8,128)(2,1)S(1)}, bf16[4,2,384,128]{3,2,1,0:T(8,128)(2,1)S(1)}, u32[]{:S(2)}, u32[]{:S(2)}) collective-permute-start(bf16[4,2,384,128]{3,2,1,0:T(8,128)(2,1)S(1)} %pad_maximum_fusion.1.refs_0_.refs_4_), channel_id=1, source_target_pairs={{0,12},{1,13},{2,14},{3,15},{4,0},{5,1},{6,2},{7,3},{8,4},{9,5},{1... | collective-permute-start | bytes 2359304 | tf_op jit(solution)/shard_map/ppermute | solution.py:53
  32.5 17.7 %collective-permute-start.8 = (bf16[4,2,384,128]{3,2,1,0:T(8,128)(2,1)S(1)}, bf16[4,2,384,128]{3,2,1,0:T(8,128)(2,1)S(1)}, u32[]{:S(2)}, u32[]{:S(2)}) collective-permute-start(bf16[4,2,384,128]{3,2,1,0:T(8,128)(2,1)S(1)} %pad_maximum_fusion.refs_0_), channel_id=1, source_target_pairs={{0,12},{1,13},{2,14},{3,15},{4,0},{5,1},{6,2},{7,3},{8,4},{9,5},{1... | collective-permute-start | bytes 2359304 | tf_op jit(solution)/shard_map/ppermute | solution.py:53
  42.1 12.3 %collective-permute-start.12 = (bf16[4,2,384,128]{3,2,1,0:T(8,128)(2,1)S(1)}, bf16[4,2,384,128]{3,2,1,0:T(8,128)(2,1)S(1)}, u32[]{:S(2)}, u32[]{:S(2)}) collective-permute-start(bf16[4,2,384,128]{3,2,1,0:T(8,128)(2,1)S(1)} %collective-permute-done.9.refs_1_.refs_5_), channel_id=1, source_target_pairs={{0,4},{1,5},{2,6},{3,7},{4,8},{5,9},{6,10},{7,11},{8,12},{9,13},{1... | collective-permute-start | bytes 2359304 | tf_op jit(solution)/shard_map/ppermute | solution.py:53
  50.2 14.2 %collective-permute-start.11 = (bf16[4,2,384,128]{3,2,1,0:T(8,128)(2,1)S(1)}, bf16[4,2,384,128]{3,2,1,0:T(8,128)(2,1)S(1)}, u32[]{:S(2)}, u32[]{:S(2)}) collective-permute-start(bf16[4,2,384,128]{3,2,1,0:T(8,128)(2,1)S(1)} %collective-permute-done.8.refs_1_.refs_3_), channel_id=1, source_target_pairs={{0,12},{1,13},{2,14},{3,15},{4,0},{5,1},{6,2},{7,3},{8,4},{9,5},{1... | collective-permute-start | bytes 2359304 | tf_op jit(solution)/shard_map/ppermute | solution.py:53
  53.2 13.2 %collective-permute-start.10 = (bf16[4,2,384,128]{3,2,1,0:T(8,128)(2,1)S(1)}, bf16[4,2,384,128]{3,2,1,0:T(8,128)(2,1)S(1)}, u32[]{:S(2)}, u32[]{:S(2)}) collective-permute-start(bf16[4,2,384,128]{3,2,1,0:T(8,128)(2,1)S(1)} %pad_maximum_fusion.refs_0_), channel_id=1, source_target_pairs={{0,4},{1,5},{2,6},{3,7},{4,8},{5,9},{6,10},{7,11},{8,12},{9,13},{1... | collective-permute-start | bytes 2359304 | tf_op jit(solution)/shard_map/ppermute | solution.py:53
  57.6 8.8 %collective-permute-start.13 = (f32[384,1024]{1,0:T(8,128)S(1)}, f32[384,1024]{1,0:T(8,128)S(1)}, u32[]{:S(2)}, u32[]{:S(2)}) collective-permute-start(f32[384,1024]{1,0:T(8,128)S(1)} %other_last.1), channel_id=1, source_target_pairs={{0,64},{1,65},{2,66},{3,67},{4,68},{5,69},{6,70},{7,71},{8,72},{9,... | collective-permute-start | bytes 4718600 | tf_op jit(solution)/shard_map/ppermute | solution.py:53
  64.4 2.0 %copy-start = (s32[192,8]{0,1:T(8,128)S(1)}, s32[192,8]{0,1:T(8,128)}, u32[]{:S(2)}) copy-start(s32[192,8]{0,1:T(8,128)} %param.9) | copy-start | bytes 18436
  85.7 6.0 %collective-permute-start.14 = (bf16[192,1024]{1,0:T(8,128)(2,1)S(1)}, bf16[192,1024]{1,0:T(8,128)(2,1)S(1)}, u32[]{:S(2)}, u32[]{:S(2)}) collective-permute-start(bf16[192,1024]{1,0:T(8,128)(2,1)S(1)} %product.1.refs_8_), channel_id=1, source_target_pairs={{0,64},{1,65},{2,66},{3,67},{4,68},{5,69},{6,70},{7,71},{8,72},{9,... | collective-permute-start | bytes 1179656 | tf_op jit(solution)/shard_map/ppermute | solution.py:53
  94.8 7.0 %collective-permute-start.15 = (bf16[4,3,128,128]{3,2,1,0:T(8,128)(2,1)S(1)}, bf16[4,3,128,128]{3,2,1,0:T(8,128)(2,1)S(1)}, u32[]{:S(2)}, u32[]{:S(2)}) collective-permute-start(bf16[4,3,128,128]{3,2,1,0:T(8,128)(2,1)S(1)} %get-tuple-element.39), channel_id=1, source_target_pairs={{0,3},{1,0},{2,1},{3,2},{4,7},{5,4},{6,5},{7,6},{8,11},{9,8},{10,9... | collective-permute-start | bytes 1179656 | tf_op jit(solution)/shard_map/ppermute | solution.py:53
  95.3 15.9 %collective-permute-start.19 = (bf16[4,3,128,128]{3,2,1,0:T(8,128)(2,1)S(1)}, bf16[4,3,128,128]{3,2,1,0:T(8,128)(2,1)S(1)}, u32[]{:S(2)}, u32[]{:S(2)}) collective-permute-start(bf16[4,3,128,128]{3,2,1,0:T(8,128)(2,1)S(1)} %get-tuple-element.50), channel_id=1, source_target_pairs={{0,1},{1,2},{2,3},{3,0},{4,5},{5,6},{6,7},{7,4},{8,9},{9,10},{10,1... | collective-permute-start | bytes 1179656 | tf_op jit(solution)/shard_map/ppermute | solution.py:53
  96.3 14.8 %collective-permute-start.20 = (bf16[4,3,128,128]{3,2,1,0:T(8,128)(2,1)S(1)}, bf16[4,3,128,128]{3,2,1,0:T(8,128)(2,1)S(1)}, u32[]{:S(2)}, u32[]{:S(2)}) collective-permute-start(bf16[4,3,128,128]{3,2,1,0:T(8,128)(2,1)S(1)} %get-tuple-element.51), channel_id=1, source_target_pairs={{0,2},{1,3},{2,0},{3,1},{4,6},{5,7},{6,4},{7,5},{8,10},{9,11},{10,... | collective-permute-start | bytes 1179656 | tf_op jit(solution)/shard_map/ppermute | solution.py:53
  100.1 13.2 %collective-permute-start.16 = (bf16[4,3,128,128]{3,2,1,0:T(8,128)(2,1)S(1)}, bf16[4,3,128,128]{3,2,1,0:T(8,128)(2,1)S(1)}, u32[]{:S(2)}, u32[]{:S(2)}) collective-permute-start(bf16[4,3,128,128]{3,2,1,0:T(8,128)(2,1)S(1)} %get-tuple-element.44), channel_id=1, source_target_pairs={{0,12},{1,13},{2,14},{3,15},{4,0},{5,1},{6,2},{7,3},{8,4},{9,5},{1... | collective-permute-start | bytes 1179656 | tf_op jit(solution)/shard_map/ppermute | solution.py:53
  101.3 15.8 %collective-permute-start.17 = (bf16[4,3,128,128]{3,2,1,0:T(8,128)(2,1)S(1)}, bf16[4,3,128,128]{3,2,1,0:T(8,128)(2,1)S(1)}, u32[]{:S(2)}, u32[]{:S(2)}) collective-permute-start(bf16[4,3,128,128]{3,2,1,0:T(8,128)(2,1)S(1)} %get-tuple-element.45), channel_id=1, source_target_pairs={{0,4},{1,5},{2,6},{3,7},{4,8},{5,9},{6,10},{7,11},{8,12},{9,13},{1... | collective-permute-start | bytes 1179656 | tf_op jit(solution)/shard_map/ppermute | solution.py:53
  101.8 15.3 %collective-permute-start.18 = (bf16[4,3,128,128]{3,2,1,0:T(8,128)(2,1)S(1)}, bf16[4,3,128,128]{3,2,1,0:T(8,128)(2,1)S(1)}, u32[]{:S(2)}, u32[]{:S(2)}) collective-permute-start(bf16[4,3,128,128]{3,2,1,0:T(8,128)(2,1)S(1)} %get-tuple-element.47), channel_id=1, source_target_pairs={{0,8},{1,9},{2,10},{3,11},{4,12},{5,13},{6,14},{7,15},{8,0},{9,1},... | collective-permute-start | bytes 1179656 | tf_op jit(solution)/shard_map/ppermute | solution.py:53
  111.4 5.7 %collective-permute-start.21 = (bf16[4,3,128,128]{3,2,1,0:T(8,128)(2,1)S(1)}, bf16[4,3,128,128]{3,2,1,0:T(8,128)(2,1)S(1)}, u32[]{:S(2)}, u32[]{:S(2)}) collective-permute-start(bf16[4,3,128,128]{3,2,1,0:T(8,128)(2,1)S(1)} %line_sum.1), channel_id=1, source_target_pairs={{0,64},{1,65},{2,66},{3,67},{4,68},{5,69},{6,70},{7,71},{8,72},{9,... | collective-permute-start | bytes 1179656 | tf_op jit(solution)/shard_map/ppermute | solution.py:53
where the time goes:
time: 134 us; the launch traced here: 133 us
  Pallas kernels  38.9 us (29%)
  starting transfers between devices  34.7 us (26%)
  blocking collectives  31.2 us (23%)
  waiting for transfers between devices  27.4 us (20%)
    ppermute x22, starting transfers between devices, permute(): return lax.ppermute(value, AXES, pairs)  34.7 us
    ppermute x22, waiting for transfers between devices, permute(): return lax.ppermute(value, AXES, pairs)  27.4 us
    all_to_all x1, blocking collectives, shards(): lax.all_to_all(jnp.broadcast_to(stats[None], (64, 8, 128)), 'vocab', spli...  16.4 us
    all_to_all x1, blocking collectives, shards(): lax.all_to_all(slab, AXES, split_axis=0, concat_axis=0, tiled=True, axis_...  14.8 us
    pallas_call x5, Pallas kernels, scores(): pl.pallas_call(functools.partial(score_kernel, steps=steps, added=added,...  13.9 us
    pallas_call x1, Pallas kernels, outer(): pl.pallas_call(outer_kernel, grid=(8,), in_specs=[SCALARS] + [rows] * 8 +...  8.49 us
    pallas_call x2, Pallas kernels, load_near(): pl.pallas_call(load_kernel, in_specs=[pl.BlockSpec(memory_space=pl.ANY)],...  6.78 us
    pallas_call x2, Pallas kernels, back(): pl.pallas_call(functools.partial(back_kernel, crossed=crossed), in_specs=...  6.18 us
  transfers between devices with their start and end apart: 22, of which 11 were waited for; matrix products, arithmetic and copies ran while one was open for 0% of the time, Pallas kernels for 22%

commit v1 on v0

--- a/solution.py
+++ b/solution.py
@@ -370,16 +370,16 @@
     tangent_head, _ = lax.optimization_barrier((tangent_head, other1))
     near = (head_near, load_near(tangent_head, "load_tangent"))
     early = scores(place, (0, 1), [other, other1], *near, "other_first", 0)
-    own, other3, own3, early = lax.optimization_barrier((own, other3, own3, early))
-    own2, own1 = permute(own3, last_shift(-1)), permute(own, last_shift(1))
+    own, early = lax.optimization_barrier((own, early))
+    own1, own2 = permute(own, last_shift(1)), permute(own3, last_shift(-1))
     owns, others = [own, own1, own2, own3], [other, other1, other2, other3]
 
     sent = scores(place, (3, 2), [other3, other2], *near, "other_last", 10, early)
     got = permute(sent, swap_pairs())
     early = scores(place, (0, 3), [own, own3], *near, "own_first", 10)
     late = (got, jnp.transpose(allowed))
-    early = scores(place, (2,), [own2], *near, "own_next", 0, early)
-    weights, tangent, stats = scores(place, (1,), [own1], *near, "own_last", 0, early, late)
+    early = scores(place, (1,), [own1], *near, "own_next", 0, early)
+    weights, tangent, stats = scores(place, (2,), [own2], *near, "own_last", 0, early, late)
     every = lax.all_to_all(
         jnp.broadcast_to(stats[None], (64, 8, 128)), "vocab", split_axis=0, concat_axis=0, tiled=True
     )

time: 134 us -> 131 us (0.978)
  starting transfers between devices: 34.7 us -> 33.2 us
    ppermute x22, starting transfers between devices: 34.7 us -> 33.2 us  [permute(): return lax.ppermute(value, AXES, pairs)]
  transfers between devices with their start and end apart: 22 -> 22, of which waited for: 11 -> 10; matrix products, arithmetic and copies ran while one was open for 0% -> 0% of each run, Pallas kernels for 22% -> 23%
where the time goes in v1:
time: 131 us
  Pallas kernels  38.9 us (30%)
  starting transfers between devices  33.2 us (25%)
  blocking collectives  30.1 us (23%)
  waiting for transfers between devices  27.6 us (21%)
    ppermute x22, starting transfers between devices, permute(): return lax.ppermute(value, AXES, pairs)  33.2 us
    ppermute x22, waiting for transfers between devices, permute(): return lax.ppermute(value, AXES, pairs)  27.6 us
    all_to_all x1, blocking collectives, shards(): lax.all_to_all(jnp.broadcast_to(stats[None], (64, 8, 128)), 'vocab', spli...  15.3 us
    all_to_all x1, blocking collectives, shards(): lax.all_to_all(slab, AXES, split_axis=0, concat_axis=0, tiled=True, axis_...  14.7 us
    pallas_call x5, Pallas kernels, scores(): pl.pallas_call(functools.partial(score_kernel, steps=steps, added=added,...  13.9 us
    pallas_call x1, Pallas kernels, outer(): pl.pallas_call(outer_kernel, grid=(8,), in_specs=[SCALARS] + [rows] * 8 +...  8.5 us
    pallas_call x2, Pallas kernels, load_near(): pl.pallas_call(load_kernel, in_specs=[pl.BlockSpec(memory_space=pl.ANY)],...  6.78 us
    pallas_call x2, Pallas kernels, back(): pl.pallas_call(functools.partial(back_kernel, crossed=crossed), in_specs=...  6.17 us
  transfers between devices with their start and end apart: 22, of which 10 were waited for; matrix products, arithmetic and copies ran while one was open for 0% of the time, Pallas kernels for 23%

profile of v1, /device:TPU:1, one launch (start us, length us, event | category | flops | bytes accessed | tf_op | source)
XLA Modules:
  0.0 131.0 jit_solution(7587238079988873133)
XLA Ops:
  0.6 0.8 join.1
  1.5 6.9 %collective-permute-start = (bf16[384,128]{1,0:T(8,128)(2,1)S(1)}, bf16[384,128]{1,0:T(8,128)(2,1)S(1)}, u32[]{:S(2)}, u32[]{:S(2)}) collective-permute-start(bf16[384,128]{1,0:T(8,128)(2,1)S(1)} %join.1), channel_id=1, source_target_pairs={{0,0},{1,1},{2,2},{3,3},{4,4},{5,5},{6,6},{7,7},{8,8},{9,9},{10,10... | collective-permute-start | bytes 294920 | tf_op jit(solution)/shard_map/ppermute | solution.py:53
  8.4 0.2 collective-permute-start.1
  8.6 0.9 collective-permute-start.3
  9.6 1.4 %collective-permute-done.refs_0_ = bf16[384,128]{1,0:T(8,128)(2,1)S(1)} collective-permute-done((bf16[384,128]{1,0:T(8,128)(2,1)S(1)}, bf16[384,128]{1,0:T(8,128)(2,1)S(1)}, u32[]{:S(2)}, u32[]{:S(2)}) %collective-permute-start) | collective-permute-done | bytes 98336 | tf_op jit(solution)/shard_map/ppermute | solution.py:53
  11.0 3.7 %collective-permute-done.1.refs_1_ = bf16[384,128]{1,0:T(8,128)(2,1)S(1)} collective-permute-done((bf16[384,128]{1,0:T(8,128)(2,1)S(1)}, bf16[384,128]{1,0:T(8,128)(2,1)S(1)}, u32[]{:S(2)}, u32[]{:S(2)}) %collective-permute-start.1) | collective-permute-done | bytes 98336 | tf_op jit(solution)/shard_map/ppermute | solution.py:53
  14.7 0.5 collective-permute-done.3.refs_3_
  15.2 0.6 arrange.1
  15.8 1.4 %collective-permute-start.4 = (bf16[2,2,384,128]{3,2,1,0:T(8,128)(2,1)S(1)}, bf16[2,2,384,128]{3,2,1,0:T(8,128)(2,1)S(1)}, u32[]{:S(2)}, u32[]{:S(2)}) collective-permute-start(bf16[2,2,384,128]{3,2,1,0:T(8,128)(2,1)S(1)} %arrange.1), channel_id=1, source_target_pairs={{0,1},{1,2},{2,3},{3,0},{4,5},{5,6},{6,7},{7,4},{8,9},{9,10},{10,1... | collective-permute-start | bytes 1179656 | tf_op jit(solution)/shard_map/ppermute | solution.py:53
  17.2 2.6 %collective-permute-start.5 = (bf16[2,2,384,128]{3,2,1,0:T(8,128)(2,1)S(1)}, bf16[2,2,384,128]{3,2,1,0:T(8,128)(2,1)S(1)}, u32[]{:S(2)}, u32[]{:S(2)}) collective-permute-start(bf16[2,2,384,128]{3,2,1,0:T(8,128)(2,1)S(1)} %arrange.1), channel_id=1, source_target_pairs={{0,2},{1,3},{2,0},{3,1},{4,6},{5,7},{6,4},{7,5},{8,10},{9,11},{10,... | collective-permute-start | bytes 1179656 | tf_op jit(solution)/shard_map/ppermute | solution.py:53
  19.8 1.1 collective-permute-start.6
  20.9 3.2 %collective-permute-done.4 = bf16[2,2,384,128]{3,2,1,0:T(8,128)(2,1)S(1)} collective-permute-done((bf16[2,2,384,128]{3,2,1,0:T(8,128)(2,1)S(1)}, bf16[2,2,384,128]{3,2,1,0:T(8,128)(2,1)S(1)}, u32[]{:S(2)}, u32[]{:S(2)}) %collective-permute-start.4) | collective-permute-done | bytes 393248 | tf_op jit(solution)/shard_map/ppermute | solution.py:53
  24.1 3.4 %load_head.1.refs_2_.refs_1_.head = bf16[4096,1024]{1,0:T(8,128)(2,1)S(1)} custom-call(bf16[4096,1024]{1,0:T(8,128)(2,1)} %a.2), custom_call_target="tpu_custom_call" | custom-call | bytes 25165824 | tf_op jit(solution)/shard_map/load_head/pallas_call | solution.py:71
  27.5 2.0 %collective-permute-done.5 = bf16[2,2,384,128]{3,2,1,0:T(8,128)(2,1)S(1)} collective-permute-done((bf16[2,2,384,128]{3,2,1,0:T(8,128)(2,1)S(1)}, bf16[2,2,384,128]{3,2,1,0:T(8,128)(2,1)S(1)}, u32[]{:S(2)}, u32[]{:S(2)}) %collective-permute-start.5) | collective-permute-done | bytes 393248 | tf_op jit(solution)/shard_map/ppermute | solution.py:53
  29.7 1.0 collective-permute-start.7
  30.8 1.8 %collective-permute-start.9 = (bf16[4,2,384,128]{3,2,1,0:T(8,128)(2,1)S(1)}, bf16[4,2,384,128]{3,2,1,0:T(8,128)(2,1)S(1)}, u32[]{:S(2)}, u32[]{:S(2)}) collective-permute-start(bf16[4,2,384,128]{3,2,1,0:T(8,128)(2,1)S(1)} %pad_maximum_fusion.refs_0_), channel_id=1, source_target_pairs={{0,12},{1,13},{2,14},{3,15},{4,0},{5,1},{6,2},{7,3},{8,4},{9,5},{1... | collective-permute-start | bytes 2359304 | tf_op jit(solution)/shard_map/ppermute | solution.py:53
  32.6 1.0 collective-permute-start.12
  33.6 8.5 %collective-permute-done.7.refs_1_.refs_5_ = bf16[4,2,384,128]{3,2,1,0:T(8,128)(2,1)S(1)} collective-permute-done((bf16[4,2,384,128]{3,2,1,0:T(8,128)(2,1)S(1)}, bf16[4,2,384,128]{3,2,1,0:T(8,128)(2,1)S(1)}, u32[]{:S(2)}, u32[]{:S(2)}) %collective-permute-start.7) | collective-permute-done | bytes 786464 | tf_op jit(solution)/shard_map/ppermute | solution.py:53
  42.1 3.4 %load_tangent.1.refs_3_.refs_2_ = bf16[4096,1024]{1,0:T(8,128)(2,1)S(1)} custom-call(bf16[4096,1024]{1,0:T(8,128)(2,1)} %a.3), custom_call_target="tpu_custom_call" | custom-call | bytes 25165824 | tf_op jit(solution)/shard_map/load_tangent/pallas_call | solution.py:71
  45.5 3.2 %other_first.1.refs_4_ = f32[384,1024]{1,0:T(8,128)S(1)} custom-call(s32[4]{0:T(128)S(1)} %pad_add_fusion.place, bf16[4,2,384,128]{3,2,1,0:T(8,128)(2,1)S(1)} %pad_maximum_fusion.1.refs_0_.refs_4_, bf16[4,2,384,128]{3,2,1,0:T(8,128)(2,1)S(1)} %collective-permute-done.7.refs_1_.refs_5_, bf16[4096,1024]{1,0:T(8,128)(2,1)S(1)} %load_head.1.refs_2_.refs_1_.head, ...), custom_call_target="tpu_custom_call" | custom-call | tf_op jit(solution)/shard_map/other_first/pallas_call | solution.py:180
  48.7 1.0 collective-permute-start.8
  49.7 1.9 %collective-permute-start.10 = (bf16[4,2,384,128]{3,2,1,0:T(8,128)(2,1)S(1)}, bf16[4,2,384,128]{3,2,1,0:T(8,128)(2,1)S(1)}, u32[]{:S(2)}, u32[]{:S(2)}) collective-permute-start(bf16[4,2,384,128]{3,2,1,0:T(8,128)(2,1)S(1)} %collective-permute-done.9.refs_1_.refs_3_), channel_id=1, source_target_pairs={{0,12},{1,13},{2,14},{3,15},{4,0},{5,1},{6,2},{7,3},{8,4},{9,5},{1... | collective-permute-start | bytes 2359304 | tf_op jit(solution)/shard_map/ppermute | solution.py:53
  51.5 2.9 %collective-permute-done.11.refs_1_.refs_6_ = bf16[4,2,384,128]{3,2,1,0:T(8,128)(2,1)S(1)} collective-permute-done((bf16[4,2,384,128]{3,2,1,0:T(8,128)(2,1)S(1)}, bf16[4,2,384,128]{3,2,1,0:T(8,128)(2,1)S(1)}, u32[]{:S(2)}, u32[]{:S(2)}) %collective-permute-start.11) | collective-permute-done | bytes 786464 | tf_op jit(solution)/shard_map/ppermute | solution.py:53
  54.5 3.2 %other_last.1 = f32[384,1024]{1,0:T(8,128)S(1)} custom-call(s32[4]{0:T(128)S(1)} %pad_add_fusion.place, bf16[4,2,384,128]{3,2,1,0:T(8,128)(2,1)S(1)} %collective-permute-done.12.refs_0_.refs_7_, bf16[4,2,384,128]{3,2,1,0:T(8,128)(2,1)S(1)} %collective-permute-done.11.refs_1_.refs_6_, bf16[4096,1024]{1,0:T(8,128)(2,1)S(1)} %load_head.1.refs_2_.refs_1_.head, ...), custom_call_target="tpu_custom_call" | custom-call | flops 48318382080 | bytes 10485760 | tf_op jit(solution)/shard_map/other_last/pallas_call | solution.py:180
  57.6 3.6 %collective-permute-start.13 = (f32[384,1024]{1,0:T(8,128)S(1)}, f32[384,1024]{1,0:T(8,128)S(1)}, u32[]{:S(2)}, u32[]{:S(2)}) collective-permute-start(f32[384,1024]{1,0:T(8,128)S(1)} %other_last.1), channel_id=1, source_target_pairs={{0,64},{1,65},{2,66},{3,67},{4,68},{5,69},{6,70},{7,71},{8,72},{9,... | collective-permute-start | bytes 4718600 | tf_op jit(solution)/shard_map/ppermute | solution.py:53
  61.2 3.2 %own_first.1.refs_3_ = f32[384,1024]{1,0:T(8,128)S(1)} custom-call(s32[4]{0:T(128)S(1)} %pad_add_fusion.place, bf16[4,2,384,128]{3,2,1,0:T(8,128)(2,1)S(1)} %pad_maximum_fusion.refs_0_, bf16[4,2,384,128]{3,2,1,0:T(8,128)(2,1)S(1)} %collective-permute-done.9.refs_1_.refs_3_, bf16[4096,1024]{1,0:T(8,128)(2,1)S(1)} %load_head.1.refs_2_.refs_1_.head, ...), custom_call_target="tpu_custom_call" | custom-call | flops 48318382080 | bytes 10485760 | tf_op jit(solution)/shard_map/own_first/pallas_call | solution.py:180
  64.4 2.0 %own_next.1.refs_3_ = f32[384,1024]{1,0:T(8,128)S(1)} custom-call(s32[4]{0:T(128)S(1)} %pad_add_fusion.place, bf16[4,2,384,128]{3,2,1,0:T(8,128)(2,1)S(1)} %collective-permute-done.8.refs_0_.refs_1_, bf16[4096,1024]{1,0:T(8,128)(2,1)S(1)} %load_head.1.refs_2_.refs_1_.head, bf16[4096,1024]{1,0:T(8,128)(2,1)S(1)} %load_tangent.1.refs_3_.refs_2_, ...), custom_call_target="tpu_custom_call" | custom-call | tf_op jit(solution)/shard_map/own_next/pallas_call | solution.py:180
  66.4 2.4 %own_last.1 = (f32[192,1024]{1,0:T(8,128)S(1)}, f32[192,1024]{1,0:T(8,128)S(1)}, f32[8,128]{1,0:T(8,128)S(1)}) custom-call(s32[4]{0:T(128)S(1)} %pad_add_fusion.place, bf16[4,2,384,128]{3,2,1,0:T(8,128)(2,1)S(1)} %collective-permute-done.10.refs_0_.refs_2_, bf16[4096,1024]{1,0:T(8,128)(2,1)S(1)} %load_head.1.refs_2_.refs_1_.head, ...), custom_call_target="tpu_custom_call" | custom-call | tf_op jit(solution)/shard_map/own_last/pallas_call | solution.py:180
  68.9 15.3 %all_to_all.10.every = f32[64,8,128]{2,1,0:T(8,128)S(1)} all-to-all(f32[64,8,128]{2,1,0:T(8,128)S(1)} %broadcast_in_dim.2), channel_id=1, replica_groups=mesh['dp'=2,'vocab'=64] {'vocab'}, dimensions={0} | all-to-all | bytes 524288 | tf_op jit(solution)/shard_map/all_to_all | solution.py:383
  84.2 0.4 product.1.refs_8_
  84.6 3.3 %collective-permute-start.14 = (bf16[192,1024]{1,0:T(8,128)(2,1)S(1)}, bf16[192,1024]{1,0:T(8,128)(2,1)S(1)}, u32[]{:S(2)}, u32[]{:S(2)}) collective-permute-start(bf16[192,1024]{1,0:T(8,128)(2,1)S(1)} %product.1.refs_8_), channel_id=1, source_target_pairs={{0,64},{1,65},{2,66},{3,67},{4,68},{5,69},{6,70},{7,71},{8,72},{9,... | collective-permute-start | bytes 1179656 | tf_op jit(solution)/shard_map/ppermute | solution.py:53
  87.9 1.3 %collective-permute-done.14.product.refs_9_ = bf16[192,1024]{1,0:T(8,128)(2,1)S(1)} collective-permute-done((bf16[192,1024]{1,0:T(8,128)(2,1)S(1)}, bf16[192,1024]{1,0:T(8,128)(2,1)S(1)}, u32[]{:S(2)}, u32[]{:S(2)}) %collective-permute-start.14) | collective-permute-done | bytes 393248 | tf_op jit(solution)/shard_map/ppermute | solution.py:53
  89.2 3.1 %back_other.1 = (bf16[4,3,128,128]{3,2,1,0:T(8,128)(2,1)S(1)}, bf16[4,3,128,128]{3,2,1,0:T(8,128)(2,1)S(1)}, bf16[4,3,128,128]{3,2,1,0:T(8,128)(2,1)S(1)}, bf16[4,3,128,128]{3,2,1,0:T(8,128)(2,1)S(1)}) custom-call(s32[4]{0:T(128)S(1)} %pad_add_fusion.place, bf16[192,1024]{1,0:T(8,128)(2,1)S(1)} %collective-permute-done.14.product.refs_9_, ...), custom_call_target="tpu_custom_call" | custom-call | flops 1610612736 | bytes 10485760 | tf_op jit(solution)/shard_map/back_other/pallas_call | solution.py:240
  92.3 0.5 collective-permute-start.15
  92.8 1.1 collective-permute-start.19
  93.9 0.6 collective-permute-start.20
  94.5 3.1 %back_own.1 = (bf16[4,3,128,128]{3,2,1,0:T(8,128)(2,1)S(1)}, bf16[4,3,128,128]{3,2,1,0:T(8,128)(2,1)S(1)}, bf16[4,3,128,128]{3,2,1,0:T(8,128)(2,1)S(1)}, bf16[4,3,128,128]{3,2,1,0:T(8,128)(2,1)S(1)}) custom-call(s32[4]{0:T(128)S(1)} %pad_add_fusion.place, bf16[192,1024]{1,0:T(8,128)(2,1)S(1)} %product.1.refs_8_, ...), custom_call_target="tpu_custom_call" | custom-call | flops 1610612736 | bytes 10485760 | tf_op jit(solution)/shard_map/back_own/pallas_call | solution.py:240
  97.6 1.3 collective-permute-start.16
  98.9 0.3 collective-permute-start.17
  99.1 0.2 collective-permute-done.15.refs_1_
  99.3 0.9 collective-permute-start.18
  100.2 8.5 %head_outer.1 = bf16[4096,1024]{1,0:T(8,128)(2,1)} custom-call(s32[4]{0:T(128)S(1)} %pad_add_fusion.place, bf16[4,2,384,128]{3,2,1,0:T(8,128)(2,1)S(1)} %pad_maximum_fusion.refs_0_, bf16[4,2,384,128]{3,2,1,0:T(8,128)(2,1)S(1)} %collective-permute-done.8.refs_0_.refs_1_, bf16[4,2,384,128]{3,2,1,0:T(8,128)(2,1)S(1)} %collective-permute-done.10.refs_0_.refs_2_, ...), custom_call_target="tpu_custom_call" | custom-call | flops 3221225472 | bytes 12582912 | tf_op jit(solution)/shard_map/head_outer/pallas_call | solution.py:343
  108.7 0.2 line_sum.1
  108.9 1.9 %collective-permute-start.21 = (bf16[4,3,128,128]{3,2,1,0:T(8,128)(2,1)S(1)}, bf16[4,3,128,128]{3,2,1,0:T(8,128)(2,1)S(1)}, u32[]{:S(2)}, u32[]{:S(2)}) collective-permute-start(bf16[4,3,128,128]{3,2,1,0:T(8,128)(2,1)S(1)} %line_sum.1), channel_id=1, source_target_pairs={{0,64},{1,65},{2,66},{3,67},{4,68},{5,69},{6,70},{7,71},{8,72},{9,... | collective-permute-start | bytes 1179656 | tf_op jit(solution)/shard_map/ppermute | solution.py:53
  110.9 3.8 %collective-permute-done.17.refs_2_ = bf16[4,3,128,128]{3,2,1,0:T(8,128)(2,1)S(1)} collective-permute-done((bf16[4,3,128,128]{3,2,1,0:T(8,128)(2,1)S(1)}, bf16[4,3,128,128]{3,2,1,0:T(8,128)(2,1)S(1)}, u32[]{:S(2)}, u32[]{:S(2)}) %collective-permute-start.17) | collective-permute-done | bytes 393248 | tf_op jit(solution)/shard_map/ppermute | solution.py:53
  114.7 0.8 pack.1
  115.5 14.7 %all_to_all.11.terms = bf16[16,192,128]{2,1,0:T(8,128)(2,1)S(1)} all-to-all(bf16[16,192,128]{2,1,0:T(8,128)(2,1)S(1)} %pack.1), channel_id=1, replica_groups={{64,80,96,112,68,84,100,116,72,88,104,120,76,92,108,124},{65,81,97,113,..., dimensions={0} | all-to-all | bytes 1572864 | tf_op jit(solution)/shard_map/all_to_all | solution.py:400
  130.2 0.8 plane_sum.1
  (23 shorter events, 0.5 us)
Async XLA Ops:
  1.5 9.6 %collective-permute-start = (bf16[384,128]{1,0:T(8,128)(2,1)S(1)}, bf16[384,128]{1,0:T(8,128)(2,1)S(1)}, u32[]{:S(2)}, u32[]{:S(2)}) collective-permute-start(bf16[384,128]{1,0:T(8,128)(2,1)S(1)} %join.1), channel_id=1, source_target_pairs={{0,0},{1,1},{2,2},{3,3},{4,4},{5,5},{6,6},{7,7},{8,8},{9,9},{10,10... | collective-permute-start | bytes 294920 | tf_op jit(solution)/shard_map/ppermute | solution.py:53
  8.4 6.3 %collective-permute-start.1 = (bf16[384,128]{1,0:T(8,128)(2,1)S(1)}, bf16[384,128]{1,0:T(8,128)(2,1)S(1)}, u32[]{:S(2)}, u32[]{:S(2)}) collective-permute-start(bf16[384,128]{1,0:T(8,128)(2,1)S(1)} %join.1), channel_id=1, source_target_pairs={{0,16},{1,17},{2,18},{3,19},{4,20},{5,21},{6,22},{7,23},{8,24},{9,... | collective-permute-start | bytes 294920 | tf_op jit(solution)/shard_map/ppermute | solution.py:53
  8.6 6.1 %collective-permute-start.2 = (bf16[384,128]{1,0:T(8,128)(2,1)S(1)}, bf16[384,128]{1,0:T(8,128)(2,1)S(1)}, u32[]{:S(2)}, u32[]{:S(2)}) collective-permute-start(bf16[384,128]{1,0:T(8,128)(2,1)S(1)} %join.1), channel_id=1, source_target_pairs={{0,32},{1,33},{2,34},{3,35},{4,36},{5,37},{6,38},{7,39},{8,40},{9,... | collective-permute-start | bytes 294920 | tf_op jit(solution)/shard_map/ppermute | solution.py:53
  8.6 6.6 %collective-permute-start.3 = (bf16[384,128]{1,0:T(8,128)(2,1)S(1)}, bf16[384,128]{1,0:T(8,128)(2,1)S(1)}, u32[]{:S(2)}, u32[]{:S(2)}) collective-permute-start(bf16[384,128]{1,0:T(8,128)(2,1)S(1)} %join.1), channel_id=1, source_target_pairs={{0,48},{1,49},{2,50},{3,51},{4,52},{5,53},{6,54},{7,55},{8,56},{9,... | collective-permute-start | bytes 294920 | tf_op jit(solution)/shard_map/ppermute | solution.py:53
  15.8 8.3 %collective-permute-start.4 = (bf16[2,2,384,128]{3,2,1,0:T(8,128)(2,1)S(1)}, bf16[2,2,384,128]{3,2,1,0:T(8,128)(2,1)S(1)}, u32[]{:S(2)}, u32[]{:S(2)}) collective-permute-start(bf16[2,2,384,128]{3,2,1,0:T(8,128)(2,1)S(1)} %arrange.1), channel_id=1, source_target_pairs={{0,1},{1,2},{2,3},{3,0},{4,5},{5,6},{6,7},{7,4},{8,9},{9,10},{10,1... | collective-permute-start | bytes 1179656 | tf_op jit(solution)/shard_map/ppermute | solution.py:53
  17.2 12.3 %collective-permute-start.5 = (bf16[2,2,384,128]{3,2,1,0:T(8,128)(2,1)S(1)}, bf16[2,2,384,128]{3,2,1,0:T(8,128)(2,1)S(1)}, u32[]{:S(2)}, u32[]{:S(2)}) collective-permute-start(bf16[2,2,384,128]{3,2,1,0:T(8,128)(2,1)S(1)} %arrange.1), channel_id=1, source_target_pairs={{0,2},{1,3},{2,0},{3,1},{4,6},{5,7},{6,4},{7,5},{8,10},{9,11},{10,... | collective-permute-start | bytes 1179656 | tf_op jit(solution)/shard_map/ppermute | solution.py:53
  19.8 9.7 %collective-permute-start.6 = (bf16[2,2,384,128]{3,2,1,0:T(8,128)(2,1)S(1)}, bf16[2,2,384,128]{3,2,1,0:T(8,128)(2,1)S(1)}, u32[]{:S(2)}, u32[]{:S(2)}) collective-permute-start(bf16[2,2,384,128]{3,2,1,0:T(8,128)(2,1)S(1)} %arrange.1), channel_id=1, source_target_pairs={{0,3},{1,0},{2,1},{3,2},{4,7},{5,4},{6,5},{7,6},{8,11},{9,8},{10,9... | collective-permute-start | bytes 1179656 | tf_op jit(solution)/shard_map/ppermute | solution.py:53
  29.7 12.4 %collective-permute-start.7 = (bf16[4,2,384,128]{3,2,1,0:T(8,128)(2,1)S(1)}, bf16[4,2,384,128]{3,2,1,0:T(8,128)(2,1)S(1)}, u32[]{:S(2)}, u32[]{:S(2)}) collective-permute-start(bf16[4,2,384,128]{3,2,1,0:T(8,128)(2,1)S(1)} %pad_maximum_fusion.1.refs_0_.refs_4_), channel_id=1, source_target_pairs={{0,4},{1,5},{2,6},{3,7},{4,8},{5,9},{6,10},{7,11},{8,12},{9,13},{1... | collective-permute-start | bytes 2359304 | tf_op jit(solution)/shard_map/ppermute | solution.py:53
  30.8 18.9 %collective-permute-start.9 = (bf16[4,2,384,128]{3,2,1,0:T(8,128)(2,1)S(1)}, bf16[4,2,384,128]{3,2,1,0:T(8,128)(2,1)S(1)}, u32[]{:S(2)}, u32[]{:S(2)}) collective-permute-start(bf16[4,2,384,128]{3,2,1,0:T(8,128)(2,1)S(1)} %pad_maximum_fusion.refs_0_), channel_id=1, source_target_pairs={{0,12},{1,13},{2,14},{3,15},{4,0},{5,1},{6,2},{7,3},{8,4},{9,5},{1... | collective-permute-start | bytes 2359304 | tf_op jit(solution)/shard_map/ppermute | solution.py:53
  32.6 18.9 %collective-permute-start.12 = (bf16[4,2,384,128]{3,2,1,0:T(8,128)(2,1)S(1)}, bf16[4,2,384,128]{3,2,1,0:T(8,128)(2,1)S(1)}, u32[]{:S(2)}, u32[]{:S(2)}) collective-permute-start(bf16[4,2,384,128]{3,2,1,0:T(8,128)(2,1)S(1)} %pad_maximum_fusion.1.refs_0_.refs_4_), channel_id=1, source_target_pairs={{0,12},{1,13},{2,14},{3,15},{4,0},{5,1},{6,2},{7,3},{8,4},{9,5},{1... | collective-permute-start | bytes 2359304 | tf_op jit(solution)/shard_map/ppermute | solution.py:53
  42.1 12.3 %collective-permute-start.11 = (bf16[4,2,384,128]{3,2,1,0:T(8,128)(2,1)S(1)}, bf16[4,2,384,128]{3,2,1,0:T(8,128)(2,1)S(1)}, u32[]{:S(2)}, u32[]{:S(2)}) collective-permute-start(bf16[4,2,384,128]{3,2,1,0:T(8,128)(2,1)S(1)} %collective-permute-done.7.refs_1_.refs_5_), channel_id=1, source_target_pairs={{0,4},{1,5},{2,6},{3,7},{4,8},{5,9},{6,10},{7,11},{8,12},{9,13},{1... | collective-permute-start | bytes 2359304 | tf_op jit(solution)/shard_map/ppermute | solution.py:53
  48.7 15.7 %collective-permute-start.8 = (bf16[4,2,384,128]{3,2,1,0:T(8,128)(2,1)S(1)}, bf16[4,2,384,128]{3,2,1,0:T(8,128)(2,1)S(1)}, u32[]{:S(2)}, u32[]{:S(2)}) collective-permute-start(bf16[4,2,384,128]{3,2,1,0:T(8,128)(2,1)S(1)} %pad_maximum_fusion.refs_0_), channel_id=1, source_target_pairs={{0,4},{1,5},{2,6},{3,7},{4,8},{5,9},{6,10},{7,11},{8,12},{9,13},{1... | collective-permute-start | bytes 2359304 | tf_op jit(solution)/shard_map/ppermute | solution.py:53
  49.7 16.7 %collective-permute-start.10 = (bf16[4,2,384,128]{3,2,1,0:T(8,128)(2,1)S(1)}, bf16[4,2,384,128]{3,2,1,0:T(8,128)(2,1)S(1)}, u32[]{:S(2)}, u32[]{:S(2)}) collective-permute-start(bf16[4,2,384,128]{3,2,1,0:T(8,128)(2,1)S(1)} %collective-permute-done.9.refs_1_.refs_3_), channel_id=1, source_target_pairs={{0,12},{1,13},{2,14},{3,15},{4,0},{5,1},{6,2},{7,3},{8,4},{9,5},{1... | collective-permute-start | bytes 2359304 | tf_op jit(solution)/shard_map/ppermute | solution.py:53
  57.6 8.8 %collective-permute-start.13 = (f32[384,1024]{1,0:T(8,128)S(1)}, f32[384,1024]{1,0:T(8,128)S(1)}, u32[]{:S(2)}, u32[]{:S(2)}) collective-permute-start(f32[384,1024]{1,0:T(8,128)S(1)} %other_last.1), channel_id=1, source_target_pairs={{0,64},{1,65},{2,66},{3,67},{4,68},{5,69},{6,70},{7,71},{8,72},{9,... | collective-permute-start | bytes 4718600 | tf_op jit(solution)/shard_map/ppermute | solution.py:53
  64.4 2.0 %copy-start = (s32[192,8]{0,1:T(8,128)S(1)}, s32[192,8]{0,1:T(8,128)}, u32[]{:S(2)}) copy-start(s32[192,8]{0,1:T(8,128)} %param.9) | copy-start | bytes 18436
  84.6 4.6 %collective-permute-start.14 = (bf16[192,1024]{1,0:T(8,128)(2,1)S(1)}, bf16[192,1024]{1,0:T(8,128)(2,1)S(1)}, u32[]{:S(2)}, u32[]{:S(2)}) collective-permute-start(bf16[192,1024]{1,0:T(8,128)(2,1)S(1)} %product.1.refs_8_), channel_id=1, source_target_pairs={{0,64},{1,65},{2,66},{3,67},{4,68},{5,69},{6,70},{7,71},{8,72},{9,... | collective-permute-start | bytes 1179656 | tf_op jit(solution)/shard_map/ppermute | solution.py:53
  92.3 7.0 %collective-permute-start.15 = (bf16[4,3,128,128]{3,2,1,0:T(8,128)(2,1)S(1)}, bf16[4,3,128,128]{3,2,1,0:T(8,128)(2,1)S(1)}, u32[]{:S(2)}, u32[]{:S(2)}) collective-permute-start(bf16[4,3,128,128]{3,2,1,0:T(8,128)(2,1)S(1)} %get-tuple-element.35), channel_id=1, source_target_pairs={{0,3},{1,0},{2,1},{3,2},{4,7},{5,4},{6,5},{7,6},{8,11},{9,8},{10,9... | collective-permute-start | bytes 1179656 | tf_op jit(solution)/shard_map/ppermute | solution.py:53
  92.8 15.9 %collective-permute-start.19 = (bf16[4,3,128,128]{3,2,1,0:T(8,128)(2,1)S(1)}, bf16[4,3,128,128]{3,2,1,0:T(8,128)(2,1)S(1)}, u32[]{:S(2)}, u32[]{:S(2)}) collective-permute-start(bf16[4,3,128,128]{3,2,1,0:T(8,128)(2,1)S(1)} %get-tuple-element.46), channel_id=1, source_target_pairs={{0,1},{1,2},{2,3},{3,0},{4,5},{5,6},{6,7},{7,4},{8,9},{9,10},{10,1... | collective-permute-start | bytes 1179656 | tf_op jit(solution)/shard_map/ppermute | solution.py:53
  93.9 14.9 %collective-permute-start.20 = (bf16[4,3,128,128]{3,2,1,0:T(8,128)(2,1)S(1)}, bf16[4,3,128,128]{3,2,1,0:T(8,128)(2,1)S(1)}, u32[]{:S(2)}, u32[]{:S(2)}) collective-permute-start(bf16[4,3,128,128]{3,2,1,0:T(8,128)(2,1)S(1)} %get-tuple-element.47), channel_id=1, source_target_pairs={{0,2},{1,3},{2,0},{3,1},{4,6},{5,7},{6,4},{7,5},{8,10},{9,11},{10,... | collective-permute-start | bytes 1179656 | tf_op jit(solution)/shard_map/ppermute | solution.py:53
  97.6 13.3 %collective-permute-start.16 = (bf16[4,3,128,128]{3,2,1,0:T(8,128)(2,1)S(1)}, bf16[4,3,128,128]{3,2,1,0:T(8,128)(2,1)S(1)}, u32[]{:S(2)}, u32[]{:S(2)}) collective-permute-start(bf16[4,3,128,128]{3,2,1,0:T(8,128)(2,1)S(1)} %get-tuple-element.40), channel_id=1, source_target_pairs={{0,12},{1,13},{2,14},{3,15},{4,0},{5,1},{6,2},{7,3},{8,4},{9,5},{1... | collective-permute-start | bytes 1179656 | tf_op jit(solution)/shard_map/ppermute | solution.py:53
  98.9 15.8 %collective-permute-start.17 = (bf16[4,3,128,128]{3,2,1,0:T(8,128)(2,1)S(1)}, bf16[4,3,128,128]{3,2,1,0:T(8,128)(2,1)S(1)}, u32[]{:S(2)}, u32[]{:S(2)}) collective-permute-start(bf16[4,3,128,128]{3,2,1,0:T(8,128)(2,1)S(1)} %get-tuple-element.41), channel_id=1, source_target_pairs={{0,4},{1,5},{2,6},{3,7},{4,8},{5,9},{6,10},{7,11},{8,12},{9,13},{1... | collective-permute-start | bytes 1179656 | tf_op jit(solution)/shard_map/ppermute | solution.py:53
  99.3 15.3 %collective-permute-start.18 = (bf16[4,3,128,128]{3,2,1,0:T(8,128)(2,1)S(1)}, bf16[4,3,128,128]{3,2,1,0:T(8,128)(2,1)S(1)}, u32[]{:S(2)}, u32[]{:S(2)}) collective-permute-start(bf16[4,3,128,128]{3,2,1,0:T(8,128)(2,1)S(1)} %get-tuple-element.43), channel_id=1, source_target_pairs={{0,8},{1,9},{2,10},{3,11},{4,12},{5,13},{6,14},{7,15},{8,0},{9,1},... | collective-permute-start | bytes 1179656 | tf_op jit(solution)/shard_map/ppermute | solution.py:53
  108.9 5.7 %collective-permute-start.21 = (bf16[4,3,128,128]{3,2,1,0:T(8,128)(2,1)S(1)}, bf16[4,3,128,128]{3,2,1,0:T(8,128)(2,1)S(1)}, u32[]{:S(2)}, u32[]{:S(2)}) collective-permute-start(bf16[4,3,128,128]{3,2,1,0:T(8,128)(2,1)S(1)} %line_sum.1), channel_id=1, source_target_pairs={{0,64},{1,65},{2,66},{3,67},{4,68},{5,69},{6,70},{7,71},{8,72},{9,... | collective-permute-start | bytes 1179656 | tf_op jit(solution)/shard_map/ppermute | solution.py:53
